TPU v7x, 256 devices: a whole 4x4x8 slice. The times are simulated.
256 devices in a mesh: dp: 2 (over core), context: 128 (over x, z, y).
Axes of the slice: x: 4, y: 4, z: 8, core: 2. Of those that a mesh axis runs over, the one named last changes fastest.
Arguments:
- query_input: float32 [2, 2048, 16384], P('dp', None, 'context'), may hold values from -6 to 6
- key_input: float32 [2, 2048, 16384], P('dp', None, 'context'), may hold values from -6 to 6
- value_input: float32 [2, 2048, 16384], P('dp', None, 'context'), may hold values from -6 to 6
- filters: float32 [2048, 16384], P('context'), may hold values from -2 to 2, as said below
- cotangent: float32 [2, 2048, 16384], P('dp', None, 'context'), may hold values from -6 to 6
Outputs:
- gated_output: float32 [2, 2048, 16384], P('dp', None, 'context')
- grad_query: float32 [2, 2048, 16384], P('dp', None, 'context')
- grad_key: float32 [2, 2048, 16384], P('dp', None, 'context')
- grad_value: float32 [2, 2048, 16384], P('dp', None, 'context')
- grad_filter: float32 [2048, 16384], P('context')
Inputs may be any that keep to these rules, and one draw needn't show every extreme that they name: `filters`: real-valued filter taps, one for each channel and lag.
All inputs are finite; a program needn't handle non-finite values.
Results may differ from a plain program's by a relative error of at most 0.000098.
Values sent between devices are 32-bit elements; how exact they have to be, the bound alone decides.
A program may use at most 128 MiB of HBM per device.

v0:
```python
import functools
import math

import jax
import jax.numpy as jnp
import ml_dtypes
import numpy as np
from jax import lax
from jax.experimental import pallas as pl
from jax.experimental.pallas import tpu as pltpu
from jax.sharding import PartitionSpec as P

MESH = pl.DeviceIdType.MESH
F32 = jnp.float32
BF16 = jnp.bfloat16
N = 128
SUB = 8
CHUNKS = 2
ROWS = 2 * SUB
LANES = 128


def halves(table):
    high = table.astype(ml_dtypes.bfloat16)
    low = (table - high.astype(np.float64)).astype(ml_dtypes.bfloat16)
    return high, low


def tables():
    steps = np.arange(N, dtype=np.float64)
    total = N * N
    outer = 2.0 * math.pi / N * (steps[:, None] + 0.25) * steps[None, :]
    twist = 2.0 * math.pi / total * (steps[:, None] + 0.25) * steps[None, :]
    inner = 2.0 * math.pi / N * ((steps[:, None] * steps[None, :]) % N)
    high, low = halves(np.concatenate([np.cos(outer), -np.sin(outer)], axis=0))
    first = np.concatenate([high, low, high], axis=1)
    high, low = halves(np.concatenate([np.cos(outer.T), -np.sin(outer.T)], axis=1) / total)
    last = np.concatenate([high, low, high], axis=1)
    cos, sin = np.cos(inner), np.sin(inner)
    ahead = np.block([[cos, -sin], [sin, cos]])
    back = np.block([[cos, sin], [-sin, cos]])
    middle = np.stack([*halves(ahead), *halves(back)])
    turn = np.stack([np.cos(twist), np.sin(twist)]).astype(np.float32)
    return first, last, middle, turn


def split(value):
    high = value.astype(BF16)
    low = (value - high.astype(F32)).astype(BF16)
    return high, low


def dot(left, right):
    return jnp.dot(left, right, preferred_element_type=F32)


def columns(value, index):
    return value[:, index * LANES : (index + 1) * LANES]


def by_inner(pairs, high, low):
    stacked = jnp.concatenate([jnp.concatenate(pair, axis=1) for pair in pairs], axis=0)
    stacked_high, stacked_low = split(stacked)
    result = dot(stacked_high, high) + dot(stacked_low, high) + dot(stacked_high, low)
    return [
        (result[i * N : (i + 1) * N, :N], result[i * N : (i + 1) * N, N:])
        for i in range(len(pairs))
    ]


def forward(signals, first, high, low, cos, sin):
    signal_high, signal_low = split(jnp.concatenate(signals, axis=1))
    mixed = dot(first, jnp.concatenate([signal_high, signal_high, signal_low], axis=0))
    pairs = []
    for i in range(len(signals)):
        re, im = columns(mixed[:N], i), columns(mixed[N:], i)
        pairs.append((re * cos + im * sin, im * cos - re * sin))
    return by_inner(pairs, high, low)


def inverse(spectra, last, high, low, cos, sin):
    turned_re, turned_im = [], []
    for re, im in by_inner(spectra, high, low):
        turned_re.append(re * cos - im * sin)
        turned_im.append(re * sin + im * cos)
    stacked = jnp.concatenate(
        [jnp.concatenate(turned_re, axis=1), jnp.concatenate(turned_im, axis=1)], axis=0
    )
    stacked_high, stacked_low = split(stacked)
    return dot(last, jnp.concatenate([stacked_high, stacked_high, stacked_low], axis=0))


def times(a, b):
    return (a[0] * b[0] - a[1] * b[1], a[0] * b[1] + a[1] * b[0])


def conj_times(a, b):
    return (a[0] * b[0] + a[1] * b[1], a[0] * b[1] - a[1] * b[0])


def exchange_kernel(
    size,
    q_hbm, k_hbm, v_hbm, c_hbm, filt_hbm, first_hbm, last_hbm, middle_hbm, turn_hbm,
    back_ref, own_ref, other_ref,
    q_ref, k_ref, v_ref, c_ref, filt_ref, first_ref, last_ref, middle_ref, turn_ref,
    send_ref, recv_ref, out_ref, spec_ref,
    load_sems, in_send, in_recv, out_send, out_recv, pair_send, pair_recv,
):
    me = lax.axis_index("context")
    pair = lax.axis_index("dp")

    def loader(i, source, target):
        return pltpu.make_async_copy(source, target, load_sems.at[i])

    loads = [
        loader(i, source, target)
        for i, (source, target) in enumerate(
            [
                (k_hbm, k_ref), (v_hbm, v_ref), (c_hbm, c_ref), (q_hbm, q_ref),
                (filt_hbm, filt_ref), (first_hbm, first_ref), (last_hbm, last_ref),
                (middle_hbm, middle_ref), (turn_hbm, turn_ref),
            ]
        )
    ]
    for load in loads:
        load.start()

    barrier = pltpu.get_barrier_semaphore()

    @pl.loop(1, size)
    def _(step):
        pl.semaphore_signal(
            barrier, inc=1, device_id=(pair, lax.rem(me + step, size)), device_id_type=MESH
        )

    pl.semaphore_signal(barrier, inc=1, device_id=(1 - pair, me), device_id_type=MESH)

    for load in loads[:4]:
        load.wait()

    def rows_of(peer):
        return pl.ds(pl.multiple_of(peer * ROWS, ROWS), ROWS)

    def products(chunk):
        @pl.loop(0, size, unroll=8)
        def _(peer):
            base = pl.multiple_of(peer * ROWS, ROWS)
            send_ref[chunk, pl.ds(base, SUB), :] = k_ref[peer, chunk] * v_ref[peer, chunk]
            send_ref[chunk, pl.ds(base + SUB, SUB), :] = c_ref[peer, chunk] * q_ref[peer, chunk]

    def send_all(chunk, source, target, send_sem, recv_sem):
        target[chunk, rows_of(me), :] = source[chunk, rows_of(me), :]

        @pl.loop(1, size)
        def _(step):
            peer = lax.rem(me + step, size)
            pltpu.make_async_remote_copy(
                src_ref=source.at[chunk, rows_of(peer), :],
                dst_ref=target.at[chunk, rows_of(me), :],
                send_sem=send_sem.at[chunk],
                recv_sem=recv_sem.at[chunk],
                device_id=(pair, peer),
                device_id_type=MESH,
            ).start()

    def await_all(chunk, ref, sem):
        part = ref.at[chunk, pl.ds(0, (size - 1) * ROWS), :]
        pltpu.make_async_copy(part, part, sem.at[chunk]).wait()

    products(0)
    pl.semaphore_wait(barrier, size)
    send_all(0, send_ref, recv_ref, in_send, in_recv)
    products(1)
    send_all(1, send_ref, recv_ref, in_send, in_recv)

    for load in loads[4:]:
        load.wait()

    def ahead(signals):
        return forward(
            signals, first_ref[...], middle_ref[0], middle_ref[1], turn_ref[0], turn_ref[1]
        )

    for chunk in range(CHUNKS):
        @pl.loop(0, SUB // 4)
        def _(step):
            at = step * 4
            signals = [filt_ref[chunk, pl.ds(at + i, N, stride=SUB), :] for i in range(4)]
            for i, (re, im) in enumerate(ahead(signals)):
                spec_ref[chunk, at + i, 0] = re
                spec_ref[chunk, at + i, 1] = im

    def convolve(chunk):
        @pl.loop(0, SUB // 2)
        def _(step):
            at = step * 2
            signals = [
                recv_ref[chunk, pl.ds(at + i + SUB * signal, N, stride=ROWS), :]
                for i in range(2)
                for signal in range(2)
            ]
            spectra = ahead(signals)
            mixed = []
            for i in range(2):
                product, grad = spectra[2 * i], spectra[2 * i + 1]
                filt = (spec_ref[chunk, at + i, 0], spec_ref[chunk, at + i, 1])
                mixed.append(times(filt, product))
                mixed.append(conj_times(filt, grad))
                mixed.append(conj_times(product, grad))
            results = inverse(
                mixed, last_ref[...], middle_ref[2], middle_ref[3], turn_ref[0], turn_ref[1]
            )
            for i in range(2):
                out_ref[chunk, pl.ds(at + i, N, stride=ROWS), :] = columns(results, 3 * i)
                out_ref[chunk, pl.ds(at + i + SUB, N, stride=ROWS), :] = columns(
                    results, 3 * i + 1
                )
                own_ref[chunk, pl.ds(at + i, N, stride=SUB), :] = columns(results, 3 * i + 2)

    def pair_copy(chunk):
        return pltpu.make_async_remote_copy(
            src_ref=own_ref.at[chunk],
            dst_ref=other_ref.at[chunk],
            send_sem=pair_send.at[chunk],
            recv_sem=pair_recv.at[chunk],
            device_id=(1 - pair, me),
            device_id_type=MESH,
        )

    for chunk in range(CHUNKS):
        await_all(chunk, recv_ref, in_recv)
        convolve(chunk)
        send_all(chunk, out_ref, back_ref, out_send, out_recv)
        pair_copy(chunk).start()

    for chunk in range(CHUNKS):
        pair_copy(chunk).wait()
        await_all(chunk, send_ref, in_send)
        await_all(chunk, out_ref, out_send)
    for chunk in range(CHUNKS):
        await_all(chunk, back_ref, out_recv)


def gate_kernel(
    scale, q_ref, k_ref, v_ref, c_ref, back_ref, own_ref, other_ref,
    gated_ref, grad_q_ref, grad_k_ref, grad_v_ref, grad_f_ref,
):
    conv, back = back_ref[0, :, 0], back_ref[0, :, 1]
    gated_ref[:, 0] = q_ref[:, 0] * conv
    grad_q_ref[:, 0] = c_ref[:, 0] * conv
    grad_k_ref[:, 0] = v_ref[:, 0] * back
    grad_v_ref[:, 0] = k_ref[:, 0] * back
    grad_f_ref[...] = (own_ref[...] + other_ref[...]) * scale


def on_device(query_input, key_input, value_input, filters, cotangent):
    size = lax.axis_size("context")
    channels = query_input.shape[1]
    rows, length = filters.shape
    scale = 1.0 / math.sqrt(lax.axis_size("dp") * length)
    token_shape = (size, CHUNKS, SUB, LANES)
    tokens = [
        array.reshape(token_shape) for array in (query_input, key_input, value_input, cotangent)
    ]
    taps = filters.reshape(CHUNKS, SUB, size, LANES).transpose(0, 2, 1, 3)
    taps = taps.reshape(CHUNKS, size * SUB, LANES)
    constants = [jnp.asarray(table) for table in tables()]

    any_spec = pl.BlockSpec(memory_space=pl.ANY)
    vmem_spec = pl.BlockSpec(memory_space=pltpu.VMEM)
    wide = (CHUNKS, size * ROWS, LANES)
    narrow = (CHUNKS, size * SUB, LANES)
    per_chunk = pltpu.SemaphoreType.DMA((CHUNKS,))
    back, own, other = pl.pallas_call(
        functools.partial(exchange_kernel, size),
        out_shape=[
            jax.ShapeDtypeStruct(wide, F32),
            jax.ShapeDtypeStruct(narrow, F32),
            jax.ShapeDtypeStruct(narrow, F32),
        ],
        in_specs=[any_spec] * 9,
        out_specs=[vmem_spec] * 3,
        scratch_shapes=[pltpu.VMEM(token_shape, F32) for _ in range(4)]
        + [pltpu.VMEM(narrow, F32)]
        + [pltpu.VMEM(table.shape, table.dtype) for table in constants]
        + [
            pltpu.VMEM(wide, F32),
            pltpu.VMEM(wide, F32),
            pltpu.VMEM(wide, F32),
            pltpu.VMEM((CHUNKS, SUB, 2, N, LANES), F32),
            pltpu.SemaphoreType.DMA((9,)),
        ]
        + [per_chunk] * 6,
        compiler_params=pltpu.CompilerParams(
            collective_id=0, has_side_effects=True, vmem_limit_bytes=40 * 2**20
        ),
        name="exchange",
    )(*tokens, taps, *constants)

    block = 32
    def token_block(i, chunk):
        return (i, chunk, 0, 0)
    token_spec = pl.BlockSpec((block, 1, SUB, LANES), token_block)
    filter_spec = pl.BlockSpec((1, block * SUB, LANES), lambda i, chunk: (chunk, i, 0))
    back_spec = pl.BlockSpec(
        (1, block, 2, SUB, LANES), lambda i, chunk: (chunk, i, 0, 0, 0)
    )
    results = pl.pallas_call(
        functools.partial(gate_kernel, scale),
        grid=(size // block, CHUNKS),
        out_shape=[jax.ShapeDtypeStruct(token_shape, F32)] * 4
        + [jax.ShapeDtypeStruct(narrow, F32)],
        in_specs=[token_spec] * 4 + [back_spec, filter_spec, filter_spec],
        out_specs=[token_spec] * 4 + [filter_spec],
        name="gate",
    )(*tokens, back.reshape(CHUNKS, size, 2, SUB, LANES), own, other)
    per_token = [array.reshape(1, channels, LANES) for array in results[:4]]
    grad_filter = results[4].reshape(CHUNKS, size, SUB, LANES).transpose(0, 2, 1, 3)
    return (*per_token, grad_filter.reshape(rows, length))


def solution(mesh):
    token = P("dp", None, "context")
    taps = P("context", None)
    return jax.shard_map(
        on_device,
        mesh=mesh,
        in_specs=(token, token, token, taps, token),
        out_specs=(token, token, token, token, taps),
        check_vma=False,
    )
```

profile of v0, /device:TPU:32, one launch (start us, length us, event | category | flops | bytes accessed | tf_op | source)
XLA Modules:
  0.0 126.9 jit_solution(1558746327437017760)
XLA Ops:
  0.6 0.0 copy-start
  0.6 1.2 copy-done
  1.9 0.0 copy-start.1
  1.9 1.2 copy-done.1
  3.1 0.0 copy-start.2
  3.1 1.2 copy-done.2
  4.3 0.0 copy-start.3
  4.3 1.2 copy-done.3
  5.5 0.0 copy-start.5
  5.5 1.2 copy-done.5
  6.8 0.0 copy-start.8
  6.8 1.0 copy-done.8
  7.8 0.0 copy-start.9
  7.8 0.9 copy-done.9
  8.7 0.0 copy-start.10
  8.7 0.9 copy-done.10
  9.7 0.0 copy-start.11
  9.7 0.9 copy-done.11
  10.6 105.1 %exchange.1 = (f32[2,2048,128]{2,1,0:T(8,128)S(1)}, f32[2,1024,128]{2,1,0:T(8,128)S(1)}, f32[2,1024,128]{2,1,0:T(8,128)S(1)}) custom-call(f32[128,2,8,128]{3,2,1,0:T(8,128)S(1)} %bitcast.20, f32[128,2,8,128]{3,2,1,0:T(8,128)S(1)} %bitcast.22, f32[128,2,8,128]{3,2,1,0:T(8,128)S(1)} %bitcast.24, f32[128,2,8,128]{3,2,1,0:T(8,128)S(1)} %bitcast.26, ...), custom_call_target="tpu_custom_call" | custom-call | tf_op jit(solution)/shard_map/exchange/pallas_call | solution.py:274
  115.7 0.0 copy-start.4
  115.7 1.3 %copy-done.4 = f32[2,2048,128]{2,1,0:T(8,128)} copy-done((f32[2,2048,128]{2,1,0:T(8,128)}, f32[2,2048,128]{2,1,0:T(8,128)S(1)}, u32[]{:S(2)}) %copy-start.4) | copy-done | bytes 2097176
  117.0 0.0 copy-start.6
  117.0 1.0 copy-done.6
  118.0 0.0 copy-start.7
  118.0 1.0 copy-done.7
  119.0 7.9 %gate.1 = (f32[128,2,8,128]{3,2,1,0:T(8,128)}, f32[128,2,8,128]{3,2,1,0:T(8,128)}, f32[128,2,8,128]{3,2,1,0:T(8,128)}, f32[128,2,8,128]{3,2,1,0:T(8,128)}, f32[2,1024,128]{2,1,0:T(8,128)}) custom-call(f32[128,2,8,128]{3,2,1,0:T(8,128)} %bitcast.19, f32[128,2,8,128]{3,2,1,0:T(8,128)} %bitcast.21, f32[128,2,8,128]{3,2,1,0:T(8,128)} %bitcast.23, ...), custom_call_target="tpu_custom_call" | custom-call | tf_op jit(solution)/shard_map/gate/pallas_call | solution.py:308
Async XLA Ops:
  0.6 1.2 copy-start
  1.9 1.2 copy-start.1
  3.1 1.2 copy-start.2
  4.3 1.2 copy-start.3
  5.5 1.2 copy-start.5
  6.8 1.0 copy-start.8
  7.8 0.9 copy-start.9
  8.7 0.9 copy-start.10
  9.7 0.9 copy-start.11
  115.7 1.3 %copy-start.4 = (f32[2,2048,128]{2,1,0:T(8,128)}, f32[2,2048,128]{2,1,0:T(8,128)S(1)}, u32[]{:S(2)}) copy-start(f32[2,2048,128]{2,1,0:T(8,128)S(1)} %get-tuple-element.13) | copy-start | bytes 6291460
  117.0 1.0 copy-start.6
  118.0 1.0 copy-start.7
where the time goes:
time: 128 us; the launch traced here: 127 us
  Pallas kernels  113 us (88%)
  local copies, waits for them, and re-layouts  13.2 us (10%)
    pallas_call x1, Pallas kernels, on_device(): pl.pallas_call(functools.partial(exchange_kernel, size), out_shape=[jax.S...  105 us
    unnamed x24, local copies, waits for them, and re-layouts  13.2 us
    pallas_call x1, Pallas kernels, on_device(): pl.pallas_call(functools.partial(gate_kernel, scale), grid=(size // block...  7.9 us

commit v1 on v0

--- a/solution.py
+++ b/solution.py
@@ -3,7 +3,6 @@
 
 import jax
 import jax.numpy as jnp
-import ml_dtypes
 import numpy as np
 from jax import lax
 from jax.experimental import pallas as pl
@@ -20,28 +19,18 @@
 LANES = 128
 
 
-def halves(table):
-    high = table.astype(ml_dtypes.bfloat16)
-    low = (table - high.astype(np.float64)).astype(ml_dtypes.bfloat16)
-    return high, low
-
-
 def tables():
     steps = np.arange(N, dtype=np.float64)
     total = N * N
     outer = 2.0 * math.pi / N * (steps[:, None] + 0.25) * steps[None, :]
     twist = 2.0 * math.pi / total * (steps[:, None] + 0.25) * steps[None, :]
     inner = 2.0 * math.pi / N * ((steps[:, None] * steps[None, :]) % N)
-    high, low = halves(np.concatenate([np.cos(outer), -np.sin(outer)], axis=0))
-    first = np.concatenate([high, low, high], axis=1)
-    high, low = halves(np.concatenate([np.cos(outer.T), -np.sin(outer.T)], axis=1) / total)
-    last = np.concatenate([high, low, high], axis=1)
+    first = np.concatenate([np.cos(outer), -np.sin(outer)], axis=0)
+    last = np.concatenate([np.cos(outer.T), -np.sin(outer.T)], axis=1) / total
     cos, sin = np.cos(inner), np.sin(inner)
-    ahead = np.block([[cos, -sin], [sin, cos]])
-    back = np.block([[cos, sin], [-sin, cos]])
-    middle = np.stack([*halves(ahead), *halves(back)])
-    turn = np.stack([np.cos(twist), np.sin(twist)]).astype(np.float32)
-    return first, last, middle, turn
+    middle = np.stack([np.block([[cos, -sin], [sin, cos]]), np.block([[cos, sin], [-sin, cos]])])
+    turn = np.stack([np.cos(twist), np.sin(twist)])
+    return [table.astype(np.float32) for table in (first, last, middle, turn)]
 
 
 def split(value):
@@ -101,13 +90,16 @@
 def exchange_kernel(
     size,
     q_hbm, k_hbm, v_hbm, c_hbm, filt_hbm, first_hbm, last_hbm, middle_hbm, turn_hbm,
-    back_ref, own_ref, other_ref,
-    q_ref, k_ref, v_ref, c_ref, filt_ref, first_ref, last_ref, middle_ref, turn_ref,
-    send_ref, recv_ref, out_ref, spec_ref,
+    back_ref, own_ref, other_ref, q_ref, k_ref, v_ref, c_ref,
+    filt_ref, first_f32, last_f32, middle_f32, turn_ref,
+    first_ref, last_ref, middle_ref, send_ref, recv_ref, out_ref, spec_ref,
     load_sems, in_send, in_recv, out_send, out_recv, pair_send, pair_recv,
 ):
     me = lax.axis_index("context")
     pair = lax.axis_index("dp")
+
+    def around(index):
+        return jnp.where(index >= size, index - size, index)
 
     def loader(i, source, target):
         return pltpu.make_async_copy(source, target, load_sems.at[i])
@@ -117,8 +109,8 @@
         for i, (source, target) in enumerate(
             [
                 (k_hbm, k_ref), (v_hbm, v_ref), (c_hbm, c_ref), (q_hbm, q_ref),
-                (filt_hbm, filt_ref), (first_hbm, first_ref), (last_hbm, last_ref),
-                (middle_hbm, middle_ref), (turn_hbm, turn_ref),
+                (filt_hbm, filt_ref), (first_hbm, first_f32), (last_hbm, last_f32),
+                (middle_hbm, middle_f32), (turn_hbm, turn_ref),
             ]
         )
     ]
@@ -127,10 +119,10 @@
 
     barrier = pltpu.get_barrier_semaphore()
 
-    @pl.loop(1, size)
+    @pl.loop(1, size, unroll=8)
     def _(step):
         pl.semaphore_signal(
-            barrier, inc=1, device_id=(pair, lax.rem(me + step, size)), device_id_type=MESH
+            barrier, inc=1, device_id=(pair, around(me + step)), device_id_type=MESH
         )
 
     pl.semaphore_signal(barrier, inc=1, device_id=(1 - pair, me), device_id_type=MESH)
@@ -153,7 +145,7 @@
 
         @pl.loop(1, size)
         def _(step):
-            peer = lax.rem(me + step, size)
+            peer = around(me + step)
             pltpu.make_async_remote_copy(
                 src_ref=source.at[chunk, rows_of(peer), :],
                 dst_ref=target.at[chunk, rows_of(me), :],
@@ -175,6 +167,15 @@
 
     for load in loads[4:]:
         load.wait()
+
+    def thirds(table):
+        high, low = split(table)
+        return jnp.concatenate([high, low, high], axis=1)
+
+    first_ref[...] = thirds(first_f32[...])
+    last_ref[...] = thirds(last_f32[...])
+    for way in range(2):
+        middle_ref[2 * way], middle_ref[2 * way + 1] = split(middle_f32[way])
 
     def ahead(signals):
         return forward(
@@ -242,15 +243,46 @@
 
 
 def gate_kernel(
-    scale, q_ref, k_ref, v_ref, c_ref, back_ref, own_ref, other_ref,
-    gated_ref, grad_q_ref, grad_k_ref, grad_v_ref, grad_f_ref,
+    scale, pieces,
+    q_ref, k_ref, v_ref, c_ref, back_ref, own_ref, other_ref,
+    gated_hbm, grad_q_hbm, grad_k_hbm, grad_v_hbm, grad_f_hbm,
+    gated_ref, grad_q_ref, grad_k_ref, grad_v_ref, grad_f_ref, sems,
 ):
-    conv, back = back_ref[0, :, 0], back_ref[0, :, 1]
-    gated_ref[:, 0] = q_ref[:, 0] * conv
-    grad_q_ref[:, 0] = c_ref[:, 0] * conv
-    grad_k_ref[:, 0] = v_ref[:, 0] * back
-    grad_v_ref[:, 0] = k_ref[:, 0] * back
-    grad_f_ref[...] = (own_ref[...] + other_ref[...]) * scale
+    block = q_ref.shape[0] // pieces
+    stores = []
+
+    def store(source, target):
+        copy = pltpu.make_async_copy(source, target, sems.at[len(stores)])
+        copy.start()
+        stores.append(copy)
+
+    for piece in range(pieces):
+        @pl.loop(piece * block, (piece + 1) * block, unroll=4)
+        def _(peer):
+            base = pl.multiple_of(peer * ROWS, ROWS)
+            for chunk in range(CHUNKS):
+                conv = back_ref[chunk, pl.ds(base, SUB), :]
+                back = back_ref[chunk, pl.ds(base + SUB, SUB), :]
+                gated_ref[peer, chunk] = q_ref[peer, chunk] * conv
+                grad_q_ref[peer, chunk] = c_ref[peer, chunk] * conv
+                grad_k_ref[peer, chunk] = v_ref[peer, chunk] * back
+                grad_v_ref[peer, chunk] = k_ref[peer, chunk] * back
+                rows = pl.ds(pl.multiple_of(peer * SUB, SUB), SUB)
+                grad_f_ref[chunk, rows, :] = (
+                    own_ref[chunk, rows, :] + other_ref[chunk, rows, :]
+                ) * scale
+
+        part = pl.ds(piece * block, block)
+        for source, target in (
+            (gated_ref, gated_hbm), (grad_q_ref, grad_q_hbm),
+            (grad_k_ref, grad_k_hbm), (grad_v_ref, grad_v_hbm),
+        ):
+            store(source.at[part], target.at[part])
+        rows = pl.ds(piece * block * SUB, block * SUB)
+        for chunk in range(CHUNKS):
+            store(grad_f_ref.at[chunk, rows, :], grad_f_hbm.at[chunk, rows, :])
+    for copy in stores:
+        copy.wait()
 
 
 def on_device(query_input, key_input, value_input, filters, cotangent):
@@ -266,24 +298,27 @@
     taps = taps.reshape(CHUNKS, size * SUB, LANES)
     constants = [jnp.asarray(table) for table in tables()]
 
-    any_spec = pl.BlockSpec(memory_space=pl.ANY)
+    hbm_spec = pl.BlockSpec(memory_space=pltpu.HBM)
     vmem_spec = pl.BlockSpec(memory_space=pltpu.VMEM)
     wide = (CHUNKS, size * ROWS, LANES)
     narrow = (CHUNKS, size * SUB, LANES)
+    token_out = jax.ShapeDtypeStruct(token_shape, F32)
+    narrow_out = jax.ShapeDtypeStruct(narrow, F32)
     per_chunk = pltpu.SemaphoreType.DMA((CHUNKS,))
-    back, own, other = pl.pallas_call(
+    def pinned(array):
+        return pltpu.with_memory_space_constraint(array, pltpu.HBM)
+
+    back, own, other, *held = pl.pallas_call(
         functools.partial(exchange_kernel, size),
-        out_shape=[
-            jax.ShapeDtypeStruct(wide, F32),
-            jax.ShapeDtypeStruct(narrow, F32),
-            jax.ShapeDtypeStruct(narrow, F32),
-        ],
-        in_specs=[any_spec] * 9,
-        out_specs=[vmem_spec] * 3,
-        scratch_shapes=[pltpu.VMEM(token_shape, F32) for _ in range(4)]
-        + [pltpu.VMEM(narrow, F32)]
+        out_shape=[pltpu.VMEM(shape, F32) for shape in [wide, narrow, narrow] + [token_shape] * 4],
+        in_specs=[hbm_spec] * 9,
+        out_specs=[vmem_spec] * 7,
+        scratch_shapes=[pltpu.VMEM(narrow, F32)]
         + [pltpu.VMEM(table.shape, table.dtype) for table in constants]
         + [
+            pltpu.VMEM((2 * N, 3 * N), BF16),
+            pltpu.VMEM((N, 6 * N), BF16),
+            pltpu.VMEM((4, 2 * N, 2 * N), BF16),
             pltpu.VMEM(wide, F32),
             pltpu.VMEM(wide, F32),
             pltpu.VMEM(wide, F32),
@@ -295,25 +330,19 @@
             collective_id=0, has_side_effects=True, vmem_limit_bytes=40 * 2**20
         ),
         name="exchange",
-    )(*tokens, taps, *constants)
-
-    block = 32
-    def token_block(i, chunk):
-        return (i, chunk, 0, 0)
-    token_spec = pl.BlockSpec((block, 1, SUB, LANES), token_block)
-    filter_spec = pl.BlockSpec((1, block * SUB, LANES), lambda i, chunk: (chunk, i, 0))
-    back_spec = pl.BlockSpec(
-        (1, block, 2, SUB, LANES), lambda i, chunk: (chunk, i, 0, 0, 0)
-    )
+    )(*map(pinned, (*tokens, taps, *constants)))
+
+    pieces = 4
     results = pl.pallas_call(
-        functools.partial(gate_kernel, scale),
-        grid=(size // block, CHUNKS),
-        out_shape=[jax.ShapeDtypeStruct(token_shape, F32)] * 4
-        + [jax.ShapeDtypeStruct(narrow, F32)],
-        in_specs=[token_spec] * 4 + [back_spec, filter_spec, filter_spec],
-        out_specs=[token_spec] * 4 + [filter_spec],
+        functools.partial(gate_kernel, scale, pieces),
+        out_shape=[token_out] * 4 + [narrow_out],
+        in_specs=[vmem_spec] * 7,
+        out_specs=[hbm_spec] * 5,
+        scratch_shapes=[pltpu.VMEM(token_shape, F32) for _ in range(4)]
+        + [pltpu.VMEM(narrow, F32), pltpu.SemaphoreType.DMA((pieces * (4 + CHUNKS),))],
+        compiler_params=pltpu.CompilerParams(vmem_limit_bytes=20 * 2**20),
         name="gate",
-    )(*tokens, back.reshape(CHUNKS, size, 2, SUB, LANES), own, other)
+    )(*held, back, own, other)
     per_token = [array.reshape(1, channels, LANES) for array in results[:4]]
     grad_filter = results[4].reshape(CHUNKS, size, SUB, LANES).transpose(0, 2, 1, 3)
     return (*per_token, grad_filter.reshape(rows, length))

time: 128 us -> 108 us (0.84)
  local copies, waits for them, and re-layouts: 13.2 us -> 0 us
  Pallas kernels: 113 us -> 107 us
    unnamed x24 -> x0, local copies, waits for them, and re-layouts: 13.2 us -> none
    pallas_call x2, Pallas kernels: 113 us -> 107 us  [the longest x1 104 us: on_device(): pl.pallas_call(functools.partial(exchange_kernel, size), out_shape=[pltpu...]
where the time goes in v1:
time: 108 us; the launch traced here: 107 us
  Pallas kernels  107 us (99%)
    pallas_call x1, Pallas kernels, on_device(): pl.pallas_call(functools.partial(exchange_kernel, size), out_shape=[pltpu...  104 us
    pallas_call x1, Pallas kernels, on_device(): pl.pallas_call(functools.partial(gate_kernel, scale, pieces), out_shape=[...  2.67 us

profile of v1, /device:TPU:32, one launch (start us, length us, event | category | flops | bytes accessed | tf_op | source)
XLA Modules:
  0.0 107.2 jit_solution(8485642689241146650)
XLA Ops:
  0.6 103.9 %exchange.1 = (f32[2,2048,128]{2,1,0:T(8,128)S(1)}, f32[2,1024,128]{2,1,0:T(8,128)S(1)}, f32[2,1024,128]{2,1,0:T(8,128)S(1)}, f32[128,2,8,128]{3,2,1,0:T(8,128)S...) custom-call(f32[128,2,8,128]{3,2,1,0:T(8,128)} %bitcast.18, ...), custom_call_target="tpu_custom_call" | custom-call | tf_op jit(solution)/shard_map/exchange/pallas_call | solution.py:311
  104.5 2.7 %gate.1 = (f32[128,2,8,128]{3,2,1,0:T(8,128)}, f32[128,2,8,128]{3,2,1,0:T(8,128)}, f32[128,2,8,128]{3,2,1,0:T(8,128)}, f32[128,2,8,128]{3,2,1,0:T(8,128)}, f32[2,1024,128]{2,1,0:T(8,128)}) custom-call(f32[128,2,8,128]{3,2,1,0:T(8,128)S(1)} %get-tuple-element.17.q_ref, f32[128,2,8,128]{3,2,1,0:T(8,128)S(1)} %get-tuple-element.18.k_ref, ...), custom_call_target="tpu_custom_call" | custom-call | tf_op jit(solution)/shard_map/gate/pallas_call | solution.py:336

commit v2 on v1

--- a/solution.py
+++ b/solution.py
@@ -17,6 +17,7 @@
 CHUNKS = 2
 ROWS = 2 * SUB
 LANES = 128
+STRIDE, LINE = 4, 8
 
 
 def tables():
@@ -87,19 +88,36 @@
     return (a[0] * b[0] + a[1] * b[1], a[0] * b[1] - a[1] * b[0])
 
 
+def gate(chunk, peer, factors, back_ref, results):
+    base = pl.multiple_of(peer * ROWS, ROWS)
+    conv = back_ref[chunk, pl.ds(base, SUB), :]
+    back = back_ref[chunk, pl.ds(base + SUB, SUB), :]
+    for factor, signal, result in zip(factors, (conv, conv, back, back), results):
+        result[peer] = factor[peer, chunk] * signal
+
+
 def exchange_kernel(
-    size,
+    size, scale,
     q_hbm, k_hbm, v_hbm, c_hbm, filt_hbm, first_hbm, last_hbm, middle_hbm, turn_hbm,
-    back_ref, own_ref, other_ref, q_ref, k_ref, v_ref, c_ref,
-    filt_ref, first_f32, last_f32, middle_f32, turn_ref,
+    back_ref, grad_f_ref, gated_ref, grad_q_ref, grad_k_ref, grad_v_ref,
+    q_ref, k_ref, v_ref, c_ref,
+    own_ref, other_ref, filt_ref, first_f32, last_f32, middle_f32, turn_ref,
     first_ref, last_ref, middle_ref, send_ref, recv_ref, out_ref, spec_ref,
-    load_sems, in_send, in_recv, out_send, out_recv, pair_send, pair_recv,
+    load_sems, wave_sem, in_send, in_recv, out_send, out_recv, pair_send, pair_recv,
 ):
     me = lax.axis_index("context")
     pair = lax.axis_index("dp")
 
-    def around(index):
-        return jnp.where(index >= size, index - size, index)
+    planes = size // LINE
+    place = lax.rem(me // STRIDE, LINE)
+    spot = me // (STRIDE * LINE) * STRIDE + lax.rem(me, STRIDE)
+
+    def peer_at(line, plane):
+        z = place + line
+        z = jnp.where(z >= LINE, z - LINE, z)
+        at = spot + plane
+        at = jnp.where(at >= planes, at - planes, at)
+        return (at // STRIDE * LINE + z) * STRIDE + lax.rem(at, STRIDE)
 
     def loader(i, source, target):
         return pltpu.make_async_copy(source, target, load_sems.at[i])
@@ -108,25 +126,40 @@
         loader(i, source, target)
         for i, (source, target) in enumerate(
             [
-                (k_hbm, k_ref), (v_hbm, v_ref), (c_hbm, c_ref), (q_hbm, q_ref),
+                (source.at[:, chunk], target.at[:, chunk])
+                for chunk in range(CHUNKS)
+                for source, target in (
+                    (k_hbm, k_ref), (v_hbm, v_ref), (c_hbm, c_ref), (q_hbm, q_ref)
+                )
+            ]
+            + [
                 (filt_hbm, filt_ref), (first_hbm, first_f32), (last_hbm, last_f32),
                 (middle_hbm, middle_f32), (turn_hbm, turn_ref),
             ]
         )
     ]
-    for load in loads:
+    for load in loads[:4]:
         load.start()
 
     barrier = pltpu.get_barrier_semaphore()
 
-    @pl.loop(1, size, unroll=8)
-    def _(step):
-        pl.semaphore_signal(
-            barrier, inc=1, device_id=(pair, around(me + step)), device_id_type=MESH
-        )
-
+    def greet(semaphore, peer):
+        pl.semaphore_signal(semaphore, inc=1, device_id=(pair, peer), device_id_type=MESH)
+
+    for plane in range(1, planes):
+        greet(barrier, peer_at(0, plane))
+    for line in (1, LINE - 1):
+        greet(barrier, peer_at(line, 0))
     pl.semaphore_signal(barrier, inc=1, device_id=(1 - pair, me), device_id_type=MESH)
-
+    for load in loads[4:]:
+        load.start()
+
+    def tell(stage):
+        for line in (1, LINE - 1):
+            greet(wave_sem.at[stage], peer_at(line, 0))
+
+    pl.semaphore_wait(barrier, planes + 2)
+    tell(0)
     for load in loads[:4]:
         load.wait()
 
@@ -140,12 +173,9 @@
             send_ref[chunk, pl.ds(base, SUB), :] = k_ref[peer, chunk] * v_ref[peer, chunk]
             send_ref[chunk, pl.ds(base + SUB, SUB), :] = c_ref[peer, chunk] * q_ref[peer, chunk]
 
-    def send_all(chunk, source, target, send_sem, recv_sem):
-        target[chunk, rows_of(me), :] = source[chunk, rows_of(me), :]
-
-        @pl.loop(1, size)
-        def _(step):
-            peer = around(me + step)
+    def sender(chunk, source, target, send_sem, recv_sem):
+        def send(line, plane):
+            peer = peer_at(line, plane)
             pltpu.make_async_remote_copy(
                 src_ref=source.at[chunk, rows_of(peer), :],
                 dst_ref=target.at[chunk, rows_of(me), :],
@@ -155,17 +185,53 @@
                 device_id_type=MESH,
             ).start()
 
+        return send
+
+    def keep(chunk, source, target):
+        target[chunk, rows_of(me), :] = source[chunk, rows_of(me), :]
+
+    def send_plane(send, line):
+        @pl.loop(0, planes)
+        def _(plane):
+            send(line, plane)
+
+    def send_own_plane(send):
+        @pl.loop(1, planes)
+        def _(plane):
+            send(0, plane)
+
+    def send_all(chunk, source, target, send_sem, recv_sem):
+        keep(chunk, source, target)
+        send = sender(chunk, source, target, send_sem, recv_sem)
+        for line in (4, 1, 7, 2, 6, 3, 5):
+            send(line, 0)
+
+        @pl.loop(1, planes)
+        def _(plane):
+            for line in (4, 1, 7, 2, 0, 6, 3, 5):
+                send(line, plane)
+
     def await_all(chunk, ref, sem):
         part = ref.at[chunk, pl.ds(0, (size - 1) * ROWS), :]
         pltpu.make_async_copy(part, part, sem.at[chunk]).wait()
 
     products(0)
-    pl.semaphore_wait(barrier, size)
-    send_all(0, send_ref, recv_ref, in_send, in_recv)
+    keep(0, send_ref, recv_ref)
+    send = sender(0, send_ref, recv_ref, in_send, in_recv)
+    for stage in range(1, LINE // 2):
+        pl.semaphore_wait(wave_sem.at[stage - 1], 2)
+        tell(stage)
+        send_plane(send, stage)
+        send_plane(send, LINE - stage)
+    pl.semaphore_wait(wave_sem.at[LINE // 2 - 1], 2)
+    send_plane(send, LINE // 2)
+    send_own_plane(send)
+    for load in loads[4:8]:
+        load.wait()
     products(1)
     send_all(1, send_ref, recv_ref, in_send, in_recv)
 
-    for load in loads[4:]:
+    for load in loads[8:]:
         load.wait()
 
     def thirds(table):
@@ -236,19 +302,32 @@
 
     for chunk in range(CHUNKS):
         pair_copy(chunk).wait()
+    grad_f_ref[...] = (own_ref[...] + other_ref[...]) * scale
+
+    await_all(0, back_ref, out_recv)
+    results = (gated_ref, grad_q_ref, grad_k_ref, grad_v_ref)
+
+    @pl.loop(0, size, unroll=4)
+    def _(peer):
+        gate(0, peer, (q_ref, c_ref, v_ref, k_ref), back_ref, results)
+
+    for chunk in range(CHUNKS):
         await_all(chunk, send_ref, in_send)
         await_all(chunk, out_ref, out_send)
-    for chunk in range(CHUNKS):
-        await_all(chunk, back_ref, out_recv)
-
-
-def gate_kernel(
-    scale, pieces,
-    q_ref, k_ref, v_ref, c_ref, back_ref, own_ref, other_ref,
+    await_all(1, back_ref, out_recv)
+
+
+def store_kernel(
+    pieces,
+    back_ref, grad_f_ref, gated_ref, grad_q_ref, grad_k_ref, grad_v_ref,
+    q_ref, k_ref, v_ref, c_ref,
     gated_hbm, grad_q_hbm, grad_k_hbm, grad_v_hbm, grad_f_hbm,
-    gated_ref, grad_q_ref, grad_k_ref, grad_v_ref, grad_f_ref, sems,
+    late_gated, late_grad_q, late_grad_k, late_grad_v, sems,
 ):
     block = q_ref.shape[0] // pieces
+    early = (gated_ref, grad_q_ref, grad_k_ref, grad_v_ref)
+    late = (late_gated, late_grad_q, late_grad_k, late_grad_v)
+    targets = (gated_hbm, grad_q_hbm, grad_k_hbm, grad_v_hbm)
     stores = []
 
     def store(source, target):
@@ -256,31 +335,17 @@
         copy.start()
         stores.append(copy)
 
+    for source, target in zip(early, targets):
+        store(source, target.at[:, 0])
+    store(grad_f_ref, grad_f_hbm)
     for piece in range(pieces):
         @pl.loop(piece * block, (piece + 1) * block, unroll=4)
         def _(peer):
-            base = pl.multiple_of(peer * ROWS, ROWS)
-            for chunk in range(CHUNKS):
-                conv = back_ref[chunk, pl.ds(base, SUB), :]
-                back = back_ref[chunk, pl.ds(base + SUB, SUB), :]
-                gated_ref[peer, chunk] = q_ref[peer, chunk] * conv
-                grad_q_ref[peer, chunk] = c_ref[peer, chunk] * conv
-                grad_k_ref[peer, chunk] = v_ref[peer, chunk] * back
-                grad_v_ref[peer, chunk] = k_ref[peer, chunk] * back
-                rows = pl.ds(pl.multiple_of(peer * SUB, SUB), SUB)
-                grad_f_ref[chunk, rows, :] = (
-                    own_ref[chunk, rows, :] + other_ref[chunk, rows, :]
-                ) * scale
+            gate(1, peer, (q_ref, c_ref, v_ref, k_ref), back_ref, late)
 
         part = pl.ds(piece * block, block)
-        for source, target in (
-            (gated_ref, gated_hbm), (grad_q_ref, grad_q_hbm),
-            (grad_k_ref, grad_k_hbm), (grad_v_ref, grad_v_hbm),
-        ):
-            store(source.at[part], target.at[part])
-        rows = pl.ds(piece * block * SUB, block * SUB)
-        for chunk in range(CHUNKS):
-            store(grad_f_ref.at[chunk, rows, :], grad_f_hbm.at[chunk, rows, :])
+        for source, target in zip(late, targets):
+            store(source.at[part], target.at[part, 1])
     for copy in stores:
         copy.wait()
 
@@ -302,18 +367,19 @@
     vmem_spec = pl.BlockSpec(memory_space=pltpu.VMEM)
     wide = (CHUNKS, size * ROWS, LANES)
     narrow = (CHUNKS, size * SUB, LANES)
-    token_out = jax.ShapeDtypeStruct(token_shape, F32)
-    narrow_out = jax.ShapeDtypeStruct(narrow, F32)
+    half = (size, SUB, LANES)
     per_chunk = pltpu.SemaphoreType.DMA((CHUNKS,))
     def pinned(array):
         return pltpu.with_memory_space_constraint(array, pltpu.HBM)
 
-    back, own, other, *held = pl.pallas_call(
-        functools.partial(exchange_kernel, size),
-        out_shape=[pltpu.VMEM(shape, F32) for shape in [wide, narrow, narrow] + [token_shape] * 4],
+    held = pl.pallas_call(
+        functools.partial(exchange_kernel, size, scale),
+        out_shape=[
+            pltpu.VMEM(shape, F32) for shape in [wide, narrow] + [half] * 4 + [token_shape] * 4
+        ],
         in_specs=[hbm_spec] * 9,
-        out_specs=[vmem_spec] * 7,
-        scratch_shapes=[pltpu.VMEM(narrow, F32)]
+        out_specs=[vmem_spec] * 10,
+        scratch_shapes=[pltpu.VMEM(narrow, F32) for _ in range(3)]
         + [pltpu.VMEM(table.shape, table.dtype) for table in constants]
         + [
             pltpu.VMEM((2 * N, 3 * N), BF16),
@@ -323,7 +389,8 @@
             pltpu.VMEM(wide, F32),
             pltpu.VMEM(wide, F32),
             pltpu.VMEM((CHUNKS, SUB, 2, N, LANES), F32),
-            pltpu.SemaphoreType.DMA((9,)),
+            pltpu.SemaphoreType.DMA((4 * CHUNKS + 5,)),
+            pltpu.SemaphoreType.REGULAR((LINE // 2,)),
         ]
         + [per_chunk] * 6,
         compiler_params=pltpu.CompilerParams(
@@ -332,17 +399,18 @@
         name="exchange",
     )(*map(pinned, (*tokens, taps, *constants)))
 
-    pieces = 4
+    pieces = 2
     results = pl.pallas_call(
-        functools.partial(gate_kernel, scale, pieces),
-        out_shape=[token_out] * 4 + [narrow_out],
-        in_specs=[vmem_spec] * 7,
+        functools.partial(store_kernel, pieces),
+        out_shape=[jax.ShapeDtypeStruct(token_shape, F32)] * 4
+        + [jax.ShapeDtypeStruct(narrow, F32)],
+        in_specs=[vmem_spec] * 10,
         out_specs=[hbm_spec] * 5,
-        scratch_shapes=[pltpu.VMEM(token_shape, F32) for _ in range(4)]
-        + [pltpu.VMEM(narrow, F32), pltpu.SemaphoreType.DMA((pieces * (4 + CHUNKS),))],
+        scratch_shapes=[pltpu.VMEM(half, F32) for _ in range(4)]
+        + [pltpu.SemaphoreType.DMA((5 + 4 * pieces,))],
         compiler_params=pltpu.CompilerParams(vmem_limit_bytes=20 * 2**20),
-        name="gate",
-    )(*held, back, own, other)
+        name="store",
+    )(*held)
     per_token = [array.reshape(1, channels, LANES) for array in results[:4]]
     grad_filter = results[4].reshape(CHUNKS, size, SUB, LANES).transpose(0, 2, 1, 3)
     return (*per_token, grad_filter.reshape(rows, length))

time: 108 us -> 107 us (level)
  no operation moved by 1% of the time
where the time goes in v2:
time: 107 us
  Pallas kernels  106 us (99%)
    pallas_call x1, Pallas kernels, on_device(): pl.pallas_call(functools.partial(exchange_kernel, size, scale), out_shape...  103 us
    pallas_call x1, Pallas kernels, on_device(): pl.pallas_call(functools.partial(store_kernel, pieces), out_shape=[jax.Sh...  2.44 us

profile of v2, /device:TPU:32, one launch (start us, length us, event | category | flops | bytes accessed | tf_op | source)
XLA Modules:
  0.0 106.5 jit_solution(5966047062554532065)
XLA Ops:
  0.6 103.4 %exchange.1 = (f32[2,2048,128]{2,1,0:T(8,128)S(1)}, f32[2,1024,128]{2,1,0:T(8,128)S(1)}, f32[128,8,128]{2,1,0:T(8,128)S(1)}, f32[128,8,128]{2,1,0:T(8,128)S(1)},...) custom-call(f32[128,2,8,128]{3,2,1,0:T(8,128)} %bitcast.18, ...), custom_call_target="tpu_custom_call" | custom-call | tf_op jit(solution)/shard_map/exchange/pallas_call | solution.py:375
  104.1 2.4 %store.1 = (f32[128,2,8,128]{3,2,1,0:T(8,128)}, f32[128,2,8,128]{3,2,1,0:T(8,128)}, f32[128,2,8,128]{3,2,1,0:T(8,128)}, f32[128,2,8,128]{3,2,1,0:T(8,128)}, f32[2,1024,128]{2,1,0:T(8,128)}) custom-call(f32[2,2048,128]{2,1,0:T(8,128)S(1)} %get-tuple-element.20.back_ref, f32[2,1024,128]{2,1,0:T(8,128)S(1)} %get-tuple-element.21.grad_f_ref, ...), custom_call_target="tpu_custom_call" | custom-call | tf_op jit(solution)/shard_map/store/pallas_call | solution.py:403

commit v3 on v2

--- a/solution.py
+++ b/solution.py
@@ -107,6 +107,7 @@
 ):
     me = lax.axis_index("context")
     pair = lax.axis_index("dp")
+    taps = pl.ds(0, size * SUB)
 
     planes = size // LINE
     place = lax.rem(me // STRIDE, LINE)
@@ -133,7 +134,7 @@
                 )
             ]
             + [
-                (filt_hbm, filt_ref), (first_hbm, first_f32), (last_hbm, last_f32),
+                (filt_hbm, filt_ref.at[:, taps, :]), (first_hbm, first_f32), (last_hbm, last_f32),
                 (middle_hbm, middle_f32), (turn_hbm, turn_ref),
             ]
         )
@@ -286,7 +287,7 @@
 
     def pair_copy(chunk):
         return pltpu.make_async_remote_copy(
-            src_ref=own_ref.at[chunk],
+            src_ref=own_ref.at[chunk, taps, :],
             dst_ref=other_ref.at[chunk],
             send_sem=pair_send.at[chunk],
             recv_sem=pair_recv.at[chunk],
@@ -302,7 +303,7 @@
 
     for chunk in range(CHUNKS):
         pair_copy(chunk).wait()
-    grad_f_ref[...] = (own_ref[...] + other_ref[...]) * scale
+    grad_f_ref[...] = (own_ref[:, taps, :] + other_ref[...]) * scale
 
     await_all(0, back_ref, out_recv)
     results = (gated_ref, grad_q_ref, grad_k_ref, grad_v_ref)
@@ -367,6 +368,8 @@
     vmem_spec = pl.BlockSpec(memory_space=pltpu.VMEM)
     wide = (CHUNKS, size * ROWS, LANES)
     narrow = (CHUNKS, size * SUB, LANES)
+    wide_strided = (CHUNKS, (size + 1) * ROWS, LANES)
+    narrow_strided = (CHUNKS, (size + 1) * SUB, LANES)
     half = (size, SUB, LANES)
     per_chunk = pltpu.SemaphoreType.DMA((CHUNKS,))
     def pinned(array):
@@ -379,15 +382,15 @@
         ],
         in_specs=[hbm_spec] * 9,
         out_specs=[vmem_spec] * 10,
-        scratch_shapes=[pltpu.VMEM(narrow, F32) for _ in range(3)]
+        scratch_shapes=[pltpu.VMEM(shape, F32) for shape in (narrow_strided, narrow, narrow_strided)]
         + [pltpu.VMEM(table.shape, table.dtype) for table in constants]
         + [
             pltpu.VMEM((2 * N, 3 * N), BF16),
             pltpu.VMEM((N, 6 * N), BF16),
             pltpu.VMEM((4, 2 * N, 2 * N), BF16),
             pltpu.VMEM(wide, F32),
-            pltpu.VMEM(wide, F32),
-            pltpu.VMEM(wide, F32),
+            pltpu.VMEM(wide_strided, F32),
+            pltpu.VMEM(wide_strided, F32),
             pltpu.VMEM((CHUNKS, SUB, 2, N, LANES), F32),
             pltpu.SemaphoreType.DMA((4 * CHUNKS + 5,)),
             pltpu.SemaphoreType.REGULAR((LINE // 2,)),

time: 107 us -> 107 us (level)
  no operation moved by 1% of the time
where the time goes in v3:
time: 107 us
  Pallas kernels  106 us (99%)
    pallas_call x1, Pallas kernels, on_device(): pl.pallas_call(functools.partial(exchange_kernel, size, scale), out_shape...  103 us
    pallas_call x1, Pallas kernels, on_device(): pl.pallas_call(functools.partial(store_kernel, pieces), out_shape=[jax.Sh...  2.44 us

profile of v3, /device:TPU:32, one launch (start us, length us, event | category | flops | bytes accessed | tf_op | source)
XLA Modules:
  0.0 106.5 jit_solution(9216278977898321022)
XLA Ops:
  0.6 103.4 %exchange.1 = (f32[2,2048,128]{2,1,0:T(8,128)S(1)}, f32[2,1024,128]{2,1,0:T(8,128)S(1)}, f32[128,8,128]{2,1,0:T(8,128)S(1)}, f32[128,8,128]{2,1,0:T(8,128)S(1)},...) custom-call(f32[128,2,8,128]{3,2,1,0:T(8,128)} %bitcast.18, ...), custom_call_target="tpu_custom_call" | custom-call | tf_op jit(solution)/shard_map/exchange/pallas_call | solution.py:378
  104.1 2.4 %store.1 = (f32[128,2,8,128]{3,2,1,0:T(8,128)}, f32[128,2,8,128]{3,2,1,0:T(8,128)}, f32[128,2,8,128]{3,2,1,0:T(8,128)}, f32[128,2,8,128]{3,2,1,0:T(8,128)}, f32[2,1024,128]{2,1,0:T(8,128)}) custom-call(f32[2,2048,128]{2,1,0:T(8,128)S(1)} %get-tuple-element.20.back_ref, f32[2,1024,128]{2,1,0:T(8,128)S(1)} %get-tuple-element.21.grad_f_ref, ...), custom_call_target="tpu_custom_call" | custom-call | tf_op jit(solution)/shard_map/store/pallas_call | solution.py:406

commit v4 on v3

--- a/solution.py
+++ b/solution.py
@@ -36,8 +36,15 @@
 
 def split(value):
     high = value.astype(BF16)
-    low = (value - high.astype(F32)).astype(BF16)
-    return high, low
+    rest = value - high.astype(F32)
+    mid = rest.astype(BF16)
+    low = (rest - mid.astype(F32)).astype(BF16)
+    return high, mid, low
+
+
+def stacked_rows(value):
+    high, mid, low = split(value)
+    return jnp.concatenate([high, high, high, mid, mid, low], axis=0)
 
 
 def dot(left, right):
@@ -48,36 +55,35 @@
     return value[:, index * LANES : (index + 1) * LANES]
 
 
-def by_inner(pairs, high, low):
+def by_inner(pairs, table):
     stacked = jnp.concatenate([jnp.concatenate(pair, axis=1) for pair in pairs], axis=0)
-    stacked_high, stacked_low = split(stacked)
-    result = dot(stacked_high, high) + dot(stacked_low, high) + dot(stacked_high, low)
+    high, mid, low = split(stacked)
+    result = dot(high, table[0]) + dot(high, table[1]) + dot(high, table[2])
+    result += dot(mid, table[0]) + dot(mid, table[1]) + dot(low, table[0])
     return [
         (result[i * N : (i + 1) * N, :N], result[i * N : (i + 1) * N, N:])
         for i in range(len(pairs))
     ]
 
 
-def forward(signals, first, high, low, cos, sin):
-    signal_high, signal_low = split(jnp.concatenate(signals, axis=1))
-    mixed = dot(first, jnp.concatenate([signal_high, signal_high, signal_low], axis=0))
+def forward(signals, first, table, cos, sin):
+    mixed = dot(first, stacked_rows(jnp.concatenate(signals, axis=1)))
     pairs = []
     for i in range(len(signals)):
         re, im = columns(mixed[:N], i), columns(mixed[N:], i)
         pairs.append((re * cos + im * sin, im * cos - re * sin))
-    return by_inner(pairs, high, low)
-
-
-def inverse(spectra, last, high, low, cos, sin):
+    return by_inner(pairs, table)
+
+
+def inverse(spectra, last, table, cos, sin):
     turned_re, turned_im = [], []
-    for re, im in by_inner(spectra, high, low):
+    for re, im in by_inner(spectra, table):
         turned_re.append(re * cos - im * sin)
         turned_im.append(re * sin + im * cos)
     stacked = jnp.concatenate(
         [jnp.concatenate(turned_re, axis=1), jnp.concatenate(turned_im, axis=1)], axis=0
     )
-    stacked_high, stacked_low = split(stacked)
-    return dot(last, jnp.concatenate([stacked_high, stacked_high, stacked_low], axis=0))
+    return dot(last, stacked_rows(stacked))
 
 
 def times(a, b):
@@ -235,18 +241,19 @@
     for load in loads[8:]:
         load.wait()
 
-    def thirds(table):
-        high, low = split(table)
-        return jnp.concatenate([high, low, high], axis=1)
-
-    first_ref[...] = thirds(first_f32[...])
-    last_ref[...] = thirds(last_f32[...])
+    def stacked_columns(table):
+        high, mid, low = split(table)
+        return jnp.concatenate([high, mid, low, high, mid, high], axis=1)
+
+    first_ref[...] = stacked_columns(first_f32[...])
+    last_ref[...] = stacked_columns(last_f32[...])
     for way in range(2):
-        middle_ref[2 * way], middle_ref[2 * way + 1] = split(middle_f32[way])
+        for i, piece in enumerate(split(middle_f32[way])):
+            middle_ref[way, i] = piece
 
     def ahead(signals):
         return forward(
-            signals, first_ref[...], middle_ref[0], middle_ref[1], turn_ref[0], turn_ref[1]
+            signals, first_ref[...], middle_ref.at[0], turn_ref[0], turn_ref[1]
         )
 
     for chunk in range(CHUNKS):
@@ -276,7 +283,7 @@
                 mixed.append(conj_times(filt, grad))
                 mixed.append(conj_times(product, grad))
             results = inverse(
-                mixed, last_ref[...], middle_ref[2], middle_ref[3], turn_ref[0], turn_ref[1]
+                mixed, last_ref[...], middle_ref.at[1], turn_ref[0], turn_ref[1]
             )
             for i in range(2):
                 out_ref[chunk, pl.ds(at + i, N, stride=ROWS), :] = columns(results, 3 * i)
@@ -385,9 +392,9 @@
         scratch_shapes=[pltpu.VMEM(shape, F32) for shape in (narrow_strided, narrow, narrow_strided)]
         + [pltpu.VMEM(table.shape, table.dtype) for table in constants]
         + [
-            pltpu.VMEM((2 * N, 3 * N), BF16),
-            pltpu.VMEM((N, 6 * N), BF16),
-            pltpu.VMEM((4, 2 * N, 2 * N), BF16),
+            pltpu.VMEM((2 * N, 6 * N), BF16),
+            pltpu.VMEM((N, 12 * N), BF16),
+            pltpu.VMEM((2, 3, 2 * N, 2 * N), BF16),
             pltpu.VMEM(wide, F32),
             pltpu.VMEM(wide_strided, F32),
             pltpu.VMEM(wide_strided, F32),

time: 107 us -> 107 us (level)
  no operation moved by 1% of the time
where the time goes in v4:
time: 107 us
  Pallas kernels  106 us (99%)
    pallas_call x1, Pallas kernels, on_device(): pl.pallas_call(functools.partial(exchange_kernel, size, scale), out_shape...  103 us
    pallas_call x1, Pallas kernels, on_device(): pl.pallas_call(functools.partial(store_kernel, pieces), out_shape=[jax.Sh...  2.44 us

profile of v4, /device:TPU:32, one launch (start us, length us, event | category | flops | bytes accessed | tf_op | source)
XLA Modules:
  0.0 106.5 jit_solution(6356570100060877498)
XLA Ops:
  0.6 103.4 %exchange.1 = (f32[2,2048,128]{2,1,0:T(8,128)S(1)}, f32[2,1024,128]{2,1,0:T(8,128)S(1)}, f32[128,8,128]{2,1,0:T(8,128)S(1)}, f32[128,8,128]{2,1,0:T(8,128)S(1)},...) custom-call(f32[128,2,8,128]{3,2,1,0:T(8,128)} %bitcast.18, ...), custom_call_target="tpu_custom_call" | custom-call | tf_op jit(solution)/shard_map/exchange/pallas_call | solution.py:385
  104.1 2.4 %store.1 = (f32[128,2,8,128]{3,2,1,0:T(8,128)}, f32[128,2,8,128]{3,2,1,0:T(8,128)}, f32[128,2,8,128]{3,2,1,0:T(8,128)}, f32[128,2,8,128]{3,2,1,0:T(8,128)}, f32[2,1024,128]{2,1,0:T(8,128)}) custom-call(f32[2,2048,128]{2,1,0:T(8,128)S(1)} %get-tuple-element.20.back_ref, f32[2,1024,128]{2,1,0:T(8,128)S(1)} %get-tuple-element.21.grad_f_ref, ...), custom_call_target="tpu_custom_call" | custom-call | tf_op jit(solution)/shard_map/store/pallas_call | solution.py:413

commit v5 on v4

--- a/solution.py
+++ b/solution.py
@@ -122,6 +122,11 @@
     def peer_at(line, plane):
         z = place + line
         z = jnp.where(z >= LINE, z - LINE, z)
+        at = spot + plane
+        at = jnp.where(at >= planes, at - planes, at)
+        return (at // STRIDE * LINE + z) * STRIDE + lax.rem(at, STRIDE)
+
+    def peer_on(z, plane):
         at = spot + plane
         at = jnp.where(at >= planes, at - planes, at)
         return (at // STRIDE * LINE + z) * STRIDE + lax.rem(at, STRIDE)
@@ -180,9 +185,9 @@
             send_ref[chunk, pl.ds(base, SUB), :] = k_ref[peer, chunk] * v_ref[peer, chunk]
             send_ref[chunk, pl.ds(base + SUB, SUB), :] = c_ref[peer, chunk] * q_ref[peer, chunk]
 
-    def sender(chunk, source, target, send_sem, recv_sem):
+    def sender(chunk, source, target, send_sem, recv_sem, find=peer_at):
         def send(line, plane):
-            peer = peer_at(line, plane)
+            peer = find(line, plane)
             pltpu.make_async_remote_copy(
                 src_ref=source.at[chunk, rows_of(peer), :],
                 dst_ref=target.at[chunk, rows_of(me), :],
@@ -207,16 +212,24 @@
         def _(plane):
             send(0, plane)
 
-    def send_all(chunk, source, target, send_sem, recv_sem):
+    def send_all(chunk, source, target, send_sem, recv_sem, last=False):
         keep(chunk, source, target)
         send = sender(chunk, source, target, send_sem, recv_sem)
         for line in (4, 1, 7, 2, 6, 3, 5):
             send(line, 0)
 
-        @pl.loop(1, planes)
-        def _(plane):
-            for line in (4, 1, 7, 2, 0, 6, 3, 5):
-                send(line, plane)
+        if last:
+            send = sender(chunk, source, target, send_sem, recv_sem, peer_on)
+            for group in ((0, 4, 1, 6, 2), (7, 3, 5)):
+                @pl.loop(1, planes)
+                def _(plane):
+                    for z in group:
+                        send(z, plane)
+        else:
+            @pl.loop(1, planes)
+            def _(plane):
+                for line in (4, 1, 7, 2, 0, 6, 3, 5):
+                    send(line, plane)
 
     def await_all(chunk, ref, sem):
         part = ref.at[chunk, pl.ds(0, (size - 1) * ROWS), :]
@@ -305,7 +318,7 @@
     for chunk in range(CHUNKS):
         await_all(chunk, recv_ref, in_recv)
         convolve(chunk)
-        send_all(chunk, out_ref, back_ref, out_send, out_recv)
+        send_all(chunk, out_ref, back_ref, out_send, out_recv, chunk == CHUNKS - 1)
         pair_copy(chunk).start()
 
     for chunk in range(CHUNKS):

time: 107 us -> 106 us (level)
  no operation moved by 1% of the time
where the time goes in v5:
time: 106 us
  Pallas kernels  105 us (99%)
    pallas_call x1, Pallas kernels, on_device(): pl.pallas_call(functools.partial(exchange_kernel, size, scale), out_shape...  103 us
    pallas_call x1, Pallas kernels, on_device(): pl.pallas_call(functools.partial(store_kernel, pieces), out_shape=[jax.Sh...  2.44 us

profile of v5, /device:TPU:32, one launch (start us, length us, event | category | flops | bytes accessed | tf_op | source)
XLA Modules:
  0.0 106.1 jit_solution(14076385131491318176)
XLA Ops:
  0.6 103.0 %exchange.1 = (f32[2,2048,128]{2,1,0:T(8,128)S(1)}, f32[2,1024,128]{2,1,0:T(8,128)S(1)}, f32[128,8,128]{2,1,0:T(8,128)S(1)}, f32[128,8,128]{2,1,0:T(8,128)S(1)},...) custom-call(f32[128,2,8,128]{3,2,1,0:T(8,128)} %bitcast.18, ...), custom_call_target="tpu_custom_call" | custom-call | tf_op jit(solution)/shard_map/exchange/pallas_call | solution.py:398
  103.6 2.4 %store.1 = (f32[128,2,8,128]{3,2,1,0:T(8,128)}, f32[128,2,8,128]{3,2,1,0:T(8,128)}, f32[128,2,8,128]{3,2,1,0:T(8,128)}, f32[128,2,8,128]{3,2,1,0:T(8,128)}, f32[2,1024,128]{2,1,0:T(8,128)}) custom-call(f32[2,2048,128]{2,1,0:T(8,128)S(1)} %get-tuple-element.20.back_ref, f32[2,1024,128]{2,1,0:T(8,128)S(1)} %get-tuple-element.21.grad_f_ref, ...), custom_call_target="tpu_custom_call" | custom-call | tf_op jit(solution)/shard_map/store/pallas_call | solution.py:426
